TPU v7x, 32 devices: a whole 2x2x4 slice. The times are simulated.
32 devices in a mesh: dp: 4 (over z), ctx: 8 (over y, x, core).
Axes of the slice: x: 2, y: 2, z: 4, core: 2. Of those that a mesh axis runs over, the one named last changes fastest.
Arguments:
- positions: int32 [3072], P('dp'), parts along dimension 0, may hold values from 0 to 6143, as said below
- queries: bfloat16 [9216, 2048], P(('dp', 'ctx')), parts along dimension 0, may hold values from -12 to 12
- keys_values: bfloat16 [9216, 1024], P(('dp', 'ctx')), parts along dimension 0, may hold values from -12 to 12
- router_weight: bfloat16 [9216], P(('dp', 'ctx')), parts along dimension 0, may hold values from 0.25 to 2
Outputs:
- attended: bfloat16 [9216, 2048], P(('dp', 'ctx')), parts along dimension 0
There are 4 independent parts, one for each index of `dp`. A program takes and returns all parts, laid end to end along the dimension named above; each array names one. Nothing has to cross between parts.
Inputs may be any that keep to these rules, and one draw needn't show every extreme that they name: Distinct and increasing. The shard of positions d * 768 to (d + 1) * 768 - 1 holds at most 288 of them, and one shard holds exactly 288; slots of device d's blocks beyond counts[d] hold data that no output reads.
All inputs are finite; a program needn't handle non-finite values.
Results may differ from a plain program's by a relative error of at most 0.0085.
Values may be sent and summed in bfloat16 or wider, within the bound.
A program may use at most 64 MiB of HBM per device.

v0:
```python
import math

import jax
import jax.numpy as jnp
from jax import lax
from jax.sharding import PartitionSpec as P

QUERY_HEADS = 16
KEY_VALUE_HEADS = 4
HEAD_SIZE = 128
SEL_DEV = 96
TOK_DEV = 768
CAP = 288


large_negative_fill = -1e30


def shard_offsets(positions, devices_ctx):
    bounds = jnp.arange(devices_ctx + 1, dtype=jnp.int32) * TOK_DEV
    return jnp.sum((positions[None, :] < bounds[:, None]).astype(jnp.int32), axis=1)


def pack_forward(arrays, offsets, my_rank, devices_ctx, pair_slots):
    my_start = offsets[my_rank]
    my_count = offsets[my_rank + 1] - my_start
    target = jnp.arange(devices_ctx, dtype=jnp.int32)[:, None]
    slot_index = jnp.arange(pair_slots, dtype=jnp.int32)[None, :]
    global_idx = (my_start // devices_ctx + slot_index) * devices_ctx + target
    local_idx = global_idx - my_start
    usable = ((local_idx >= 0) & (local_idx < my_count)).reshape(-1)
    picked = jnp.clip(local_idx, 0, CAP - 1).reshape(-1)
    result = []
    for member in arrays:
        gathered_rows = jnp.take(member, picked, axis=0)
        mask_shape = usable.reshape(usable.shape + (1,) * (gathered_rows.ndim - 1))
        gathered_rows = jnp.where(mask_shape, gathered_rows, jnp.zeros_like(gathered_rows))
        result.append(gathered_rows.reshape((devices_ctx, pair_slots) + member.shape[1:]))
    return tuple(result)


def unpack_forward(received, offsets, my_rank, devices_ctx, pair_slots):
    slot_ids = jnp.arange(SEL_DEV, dtype=jnp.int32)
    global_idx = slot_ids * devices_ctx + my_rank
    owners = jnp.sum((offsets[None, 1:] <= global_idx[:, None]).astype(jnp.int32), axis=1)
    slot_index = slot_ids - jnp.take(offsets, owners) // devices_ctx
    picked = owners * pair_slots + slot_index
    return tuple(
        (jnp.take(member.reshape((-1,) + member.shape[2:]), picked, axis=0) for member in received)
    )


def pack_return(scaled, offsets, my_rank, devices_ctx, pair_slots):
    starts = offsets[:-1][:, None]
    ends = offsets[1:][:, None]
    slot_index = jnp.arange(pair_slots, dtype=jnp.int32)[None, :]
    local_idx = starts // devices_ctx + slot_index
    global_idx = local_idx * devices_ctx + my_rank
    usable = ((local_idx < SEL_DEV) & (global_idx >= starts) & (global_idx < ends)).reshape(-1)
    picked = jnp.clip(local_idx, 0, SEL_DEV - 1).reshape(-1)
    gathered_rows = jnp.take(scaled, picked, axis=0)
    gathered_rows = jnp.where(usable[:, None], gathered_rows, jnp.zeros_like(gathered_rows))
    return gathered_rows.reshape(devices_ctx, pair_slots, scaled.shape[1])


def unpack_return(received, offsets, my_rank, devices_ctx, pair_slots):
    my_start = offsets[my_rank]
    my_count = offsets[my_rank + 1] - my_start
    slot_ids = jnp.arange(CAP, dtype=jnp.int32)
    global_idx = my_start + slot_ids
    live_slot = slot_ids < my_count
    source = global_idx % devices_ctx
    slot_index = jnp.clip(global_idx // devices_ctx - my_start // devices_ctx, 0, pair_slots - 1)
    flat = received.reshape(-1, received.shape[2])
    gathered_rows = jnp.take(flat, source * pair_slots + slot_index, axis=0)
    return jnp.where(live_slot[:, None], gathered_rows, jnp.zeros_like(gathered_rows))


def block_divisions(rows_total):
    for num_blocks in range(1, rows_total + 1):
        if rows_total % num_blocks == 0 and rows_total // num_blocks <= 512:
            return num_blocks
    return rows_total


def attend(query_row_count, query_index, kv_bal, devices_ctx):
    query_row_total = query_row_count.shape[0]
    group_count = QUERY_HEADS // KEY_VALUE_HEADS
    grouped_heads = query_row_count.reshape(
        query_row_total, KEY_VALUE_HEADS, group_count, HEAD_SIZE
    )
    score_scale = 1.0 / math.sqrt(HEAD_SIZE)

    def update(running, key_block_start, block_start):
        max_run, total_run, accum = running
        key_total_count = key_block_start.shape[0]
        key_rows = block_start + jnp.arange(key_total_count, dtype=jnp.int32)
        key_index = key_rows % SEL_DEV * devices_ctx + key_rows // SEL_DEV
        block_key_rows = key_block_start[:, : KEY_VALUE_HEADS * HEAD_SIZE].reshape(
            key_total_count, KEY_VALUE_HEADS, HEAD_SIZE
        )
        block_value_rows = key_block_start[:, KEY_VALUE_HEADS * HEAD_SIZE :].reshape(
            key_total_count, KEY_VALUE_HEADS, HEAD_SIZE
        )
        scores = (
            jnp.einsum(
                "qkgd,ckd->kgqc", grouped_heads, block_key_rows, preferred_element_type=jnp.float32
            )
            * score_scale
        )
        visible = key_index[None, :] <= query_index[:, None]
        scores = jnp.where(visible, scores, large_negative_fill)
        max_new = jnp.maximum(max_run, jnp.max(scores, axis=-1))
        weights = jnp.where(visible, jnp.exp(scores - max_new[..., None]), 0.0)
        factor = jnp.exp(max_run - max_new)
        total_new = total_run * factor + jnp.sum(weights, axis=-1)
        weighted = jnp.einsum(
            "kgqc,ckd->qkgd",
            weights.astype(jnp.bfloat16),
            block_value_rows,
            preferred_element_type=jnp.float32,
        )
        accum_new = accum * jnp.transpose(factor, (2, 0, 1))[..., None] + weighted
        return (max_new, total_new, accum_new)

    def fold_piece(running, piece_rows, piece_start):
        num_blocks = block_divisions(piece_rows.shape[0])
        if num_blocks == 1:
            return update(running, piece_rows, piece_start)
        block_rows = piece_rows.shape[0] // num_blocks
        blocks = piece_rows.reshape(num_blocks, block_rows, piece_rows.shape[1])

        def scan_step(running_in, inputs_in):
            key_block_start, order_id = inputs_in
            return (update(running_in, key_block_start, piece_start + order_id * block_rows), None)

        running_out, unused = lax.scan(
            scan_step, running, (blocks, jnp.arange(num_blocks, dtype=jnp.int32))
        )
        return running_out

    initial = (
        jnp.full((KEY_VALUE_HEADS, group_count, query_row_total), large_negative_fill, jnp.float32),
        jnp.zeros((KEY_VALUE_HEADS, group_count, query_row_total), jnp.float32),
        jnp.zeros((query_row_total, KEY_VALUE_HEADS, group_count, HEAD_SIZE), jnp.float32),
    )
    max_run, total_run, accum = fold_piece(
        initial, lax.all_gather(kv_bal, "ctx", axis=0, tiled=True), jnp.int32(0)
    )
    result = accum / jnp.transpose(total_run, (2, 0, 1))[..., None]
    return result.reshape(query_row_total, QUERY_HEADS * HEAD_SIZE)


def per_device(positions, queries, keys_values, router_weight):
    devices_ctx = lax.axis_size("ctx")
    my_rank = lax.axis_index("ctx")
    pair_slots = (CAP + devices_ctx - 1) // devices_ctx + 1
    offsets = shard_offsets(positions, devices_ctx)
    packed = pack_forward(
        (queries, keys_values, router_weight), offsets, my_rank, devices_ctx, pair_slots
    )
    moved = (
        lax.all_to_all(packed[0], "ctx", split_axis=0, concat_axis=0, tiled=True),
        lax.all_to_all(packed[1], "ctx", split_axis=0, concat_axis=0, tiled=True),
        lax.all_to_all(packed[2], "ctx", split_axis=0, concat_axis=0, tiled=True),
    )
    query_bal, kv_bal, gate_bal = unpack_forward(moved, offsets, my_rank, devices_ctx, pair_slots)
    query_index = jnp.arange(SEL_DEV, dtype=jnp.int32) * devices_ctx + my_rank
    attended = attend(query_bal, query_index, kv_bal, devices_ctx)
    scaled = (gate_bal.astype(jnp.float32)[:, None] * attended).astype(jnp.bfloat16)
    outgoing = pack_return(scaled, offsets, my_rank, devices_ctx, pair_slots)
    returned = lax.all_to_all(outgoing, "ctx", split_axis=0, concat_axis=0, tiled=True)
    return unpack_return(returned, offsets, my_rank, devices_ctx, pair_slots)


def solution(mesh):
    in_specs = (P("dp"), P(("dp", "ctx"), None), P(("dp", "ctx"), None), P(("dp", "ctx")))
    out_specs = P(("dp", "ctx"), None)
    return jax.shard_map(
        per_device, mesh=mesh, in_specs=in_specs, out_specs=out_specs, check_vma=False
    )
```

profile of v0, /device:TPU:0, one launch (start us, length us, event | category | flops | bytes accessed | tf_op | source)
XLA Modules:
  0.0 146.9 jit_solution(39540964473852603)
XLA Ops:
  13.1 3.6 %gather_fusion = bf16[296]{0:T(512)(128)(2,1)S(1)} fusion(bf16[288]{0:T(512)(128)(2,1)} %param.9, s32[1024]{0:T(1024)S(1)} %pad_clamp_fusion.3), kind=kCustom, calls=%fused_computation | custom fusion | bytes 2368 | tf_op jit(solution)/shard_map/jit(_take)/gather | solution.py:35
  18.1 5.2 %all-to-all-start = ((bf16[8,1,37]{2,1,0:T(2,128)(2,1)}), bf16[8,1,37]{2,1,0:T(2,128)(2,1)S(1)}, u32[]{:S(2)}, u32[]{:S(2)}) async-start(bf16[8,1,37]{2,1,0:T(2,128)(2,1)} %copy.20), calls=%async_computation | async-start | bytes 8192 | tf_op jit(solution)/shard_map/all_to_all | solution.py:165
  24.0 2.1 %gather_fusion.2 = bf16[296,1024]{1,0:T(8,128)(2,1)S(1)} fusion(bf16[288,1024]{1,0:T(8,128)(2,1)S(1)} %copy-done.1, s32[1024]{0:T(1024)S(1)} %pad_clamp_fusion.3), kind=kCustom, calls=%fused_computation.2 | custom fusion | bytes 1213600 | tf_op jit(solution)/shard_map/jit(_take)/gather | solution.py:35
  27.9 3.7 %all-to-all-start.1 = ((bf16[8,37,1024]{2,1,0:T(8,128)(2,1)}), bf16[8,37,1024]{2,1,0:T(8,128)(2,1)S(1)}, u32[]{:S(2)}, u32[]{:S(2)}) async-start(bf16[8,37,1024]{2,1,0:T(8,128)(2,1)} %select_select_fusion.3), calls=%async_computation.1 | async-start | bytes 1310720 | tf_op jit(solution)/shard_map/all_to_all | solution.py:164
  31.7 5.5 %fusion.54 = (s32[96]{0:T(128)S(1)}, s32[96]{0:T(128)S(1)}) fusion(s32[96]{0:T(128)S(1)} %convert_reduce_fusion.1, s32[]{:T(128)} %bitcast.13, s32[]{:T(128)} %bitcast.12, s32[]{:T(128)} %bitcast.11, s32[]{:T(128)} %bitcast.10, s32[]{:T(128)} %bitcast.9, s32[]{:T(128)} %bitcast.8, s32[]{:T(128)} %bitcast.7, s32[]{:T(128)} %bitcast.6, s32[]{:T(128)} %bitcast.4), kind=kLoop, calls=%fused_computation.142 | loop fusion | flops 4224 | bytes 1188 | tf_op jit(solution)/shard_map/jit(_take)/jit(_where)/select_n | solution.py:49
  39.2 3.6 %all-to-all-done.1 = bf16[8,37,1024]{2,1,0:T(8,128)(2,1)S(1)} async-done(((bf16[8,37,1024]{2,1,0:T(8,128)(2,1)}), bf16[8,37,1024]{2,1,0:T(8,128)(2,1)S(1)}, u32[]{:S(2)}, u32[]{:S(2)}) %all-to-all-start.1) | async-done | bytes 606240 | tf_op jit(solution)/shard_map/all_to_all | solution.py:164
  44.5 3.0 %gather_fusion.4 = bf16[296,2048]{1,0:T(8,128)(2,1)} fusion(bf16[288,2048]{1,0:T(8,128)(2,1)S(1)} %copy-done, s32[1024]{0:T(1024)S(1)} %pad_clamp_fusion.3), kind=kCustom, calls=%fused_computation.4 | custom fusion | bytes 2426016 | tf_op jit(solution)/shard_map/jit(_take)/gather | solution.py:35
  47.5 1.7 %gather.57 = bf16[8,37,2048]{2,1,0:T(8,128)(2,1)S(1)} reshape(bf16[296,2048]{1,0:T(8,128)(2,1)} %gather_fusion.4) | data formatting | bytes 2424832 | tf_op jit(solution)/shard_map/jit(_take)/gather | solution.py:35
  49.2 1.3 select_select_fusion.1
  50.5 4.5 %all-to-all-start.2 = ((bf16[8,37,2048]{2,1,0:T(8,128)(2,1)}), bf16[8,37,2048]{2,1,0:T(8,128)(2,1)}, u32[]{:S(2)}, u32[]{:S(2)}) async-start(bf16[8,37,2048]{2,1,0:T(8,128)(2,1)} %select_select_fusion.1), calls=%async_computation.2 | async-start | bytes 2621440 | tf_op jit(solution)/shard_map/all_to_all | solution.py:163
  56.4 20.8 %all-to-all-done.2 = bf16[8,37,2048]{2,1,0:T(8,128)(2,1)} async-done(((bf16[8,37,2048]{2,1,0:T(8,128)(2,1)}), bf16[8,37,2048]{2,1,0:T(8,128)(2,1)}, u32[]{:S(2)}, u32[]{:S(2)}) %all-to-all-start.2) | async-done | bytes 1212448 | tf_op jit(solution)/shard_map/all_to_all | solution.py:163
  77.2 1.7 %reshape.582 = bf16[296,2048]{1,0:T(8,128)(2,1)S(1)} reshape(bf16[8,37,2048]{2,1,0:T(8,128)(2,1)} %all-to-all-done.2) | data formatting | bytes 2424832 | tf_op jit(solution)/shard_map/reshape | solution.py:49
  81.4 20.4 %while.17 = (s32[]{:T(128)}, f32[4,4,96]{2,1,0:T(4,128)S(1)}, f32[4,4,96]{2,1,0:T(4,128)}, f32[96,4,4,128]{3,0,2,1:T(8,128)}, s32[2]{0:T(128)}, /*index=5*/bf16[...) while((s32[]{:T(128)}, f32[4,4,96]{2,1,0:T(4,128)S(1)}, ...), condition=%wide.region_5.6_spmd.clone, body=%wide.region_2.5_spmd.clone.sunk | while | flops 310299456 | bytes 16715817 | solution.py:137
  87.2 2.7 %fusion.83 = f32[96,4,4,128]{3,0,2,1:T(8,128)} fusion(bf16[384,4,128,1]{0,2,3,1:T(8,128)(2,1)} %bitcast.103, f32[4,384,96,4]{1,2,3,0:T(8,128)S(1)} %get-tuple-element.268, f32[4,4,96]{2,1,0:T(4,128)S(1)} %get-tuple-element.294, pred[96,384]{1,0:T(8,128)(4,1)} %broadcast_compare_fusion.2, f32[96,4,4,128]{3,0,2,1:T(8,128)} %get-tuple-element.285, ...), kind=kOutput, calls=%fused_computation.15.clone.1 | convolution fusion | flops 154533888 | bytes 4374529 | tf_op jit(solution)/shard_map/while/body/eval_jaxpr/kgqc,ckd->qkgd/dot_general | solution.py:117
  97.3 3.0 %fusion.83 = f32[96,4,4,128]{3,0,2,1:T(8,128)} fusion(bf16[384,4,128,1]{0,2,3,1:T(8,128)(2,1)} %bitcast.103, f32[4,384,96,4]{1,2,3,0:T(8,128)S(1)} %get-tuple-element.268, f32[4,4,96]{2,1,0:T(4,128)S(1)} %get-tuple-element.294, pred[96,384]{1,0:T(8,128)(4,1)} %broadcast_compare_fusion.2, f32[96,4,4,128]{3,0,2,1:T(8,128)} %get-tuple-element.285, ...), kind=kOutput, calls=%fused_computation.15.clone.1 | convolution fusion | flops 154533888 | bytes 4374529 | tf_op jit(solution)/shard_map/while/body/eval_jaxpr/kgqc,ckd->qkgd/dot_general | solution.py:117
  101.9 1.4 broadcast_divide_fusion
  104.5 3.0 %gather_fusion.6 = bf16[296,2048]{1,0:T(8,128)(2,1)} fusion(bf16[96,2048]{1,0:T(8,128)(2,1)S(1)} %multiply_convert_fusion, s32[1024]{0:T(1024)S(1)} %copy-done.7), kind=kCustom, calls=%fused_computation.6 | custom fusion | bytes 2426016 | tf_op jit(solution)/shard_map/jit(_take)/gather | solution.py:61
  107.4 1.7 %gather.61 = bf16[8,37,2048]{2,1,0:T(8,128)(2,1)S(1)} reshape(bf16[296,2048]{1,0:T(8,128)(2,1)} %gather_fusion.6) | data formatting | bytes 2424832 | tf_op jit(solution)/shard_map/jit(_take)/gather | solution.py:61
  109.1 1.3 select_select_fusion
  110.4 4.3 %all-to-all-start.3 = ((bf16[8,37,2048]{2,1,0:T(8,128)(2,1)}), bf16[8,37,2048]{2,1,0:T(8,128)(2,1)}, u32[]{:S(2)}, u32[]{:S(2)}) async-start(bf16[8,37,2048]{2,1,0:T(8,128)(2,1)} %select_select_fusion), calls=%async_computation.3 | async-start | bytes 2621440 | tf_op jit(solution)/shard_map/all_to_all | solution.py:172
  116.1 16.8 %all-to-all-done.3 = bf16[8,37,2048]{2,1,0:T(8,128)(2,1)} async-done(((bf16[8,37,2048]{2,1,0:T(8,128)(2,1)}), bf16[8,37,2048]{2,1,0:T(8,128)(2,1)}, u32[]{:S(2)}, u32[]{:S(2)}) %all-to-all-start.3) | async-done | bytes 1212448 | tf_op jit(solution)/shard_map/all_to_all | solution.py:172
  132.9 1.7 %reshape.584 = bf16[296,2048]{1,0:T(8,128)(2,1)S(1)} reshape(bf16[8,37,2048]{2,1,0:T(8,128)(2,1)} %all-to-all-done.3) | data formatting | bytes 2424832 | tf_op jit(solution)/shard_map/reshape | solution.py:74
  134.6 3.0 %gather_fusion.7 = bf16[288,2048]{1,0:T(8,128)(2,1)} fusion(bf16[296,2048]{1,0:T(8,128)(2,1)S(1)} %reshape.584, s32[1024]{0:T(1024)S(1)} %pad_clamp_fusion), kind=kCustom, calls=%fused_computation.7 | custom fusion | bytes 2360448 | tf_op jit(solution)/shard_map/jit(_take)/gather | solution.py:75
  137.6 2.5 %select_select_fusion.2 = bf16[288,2048]{1,0:T(8,128)(2,1)} fusion(bf16[288,2048]{1,0:T(8,128)(2,1)} %gather_fusion.7, pred[288]{0:T(512)(128)(4,1)S(1)} %compare_and_fusion.3, pred[288]{0:T(512)(128)(4,1)S(1)} %iota_compare_fusion), kind=kLoop, calls=%fused_computation.46 | loop fusion | flops 1179648 | bytes 2359872 | tf_op jit(solution)/shard_map/jit(_where)/select_n | solution.py:76
  (104 shorter events, 30.0 us)
Async XLA Ops:
  6.5 38.0 %copy-start = (bf16[288,2048]{1,0:T(8,128)(2,1)S(1)}, bf16[288,2048]{1,0:T(8,128)(2,1)}, u32[]{:S(2)}) copy-start(bf16[288,2048]{1,0:T(8,128)(2,1)} %param.7) | copy-start | bytes 3538948
  6.5 17.5 %copy-start.1 = (bf16[288,1024]{1,0:T(8,128)(2,1)S(1)}, bf16[288,1024]{1,0:T(8,128)(2,1)}, u32[]{:S(2)}) copy-start(bf16[288,1024]{1,0:T(8,128)(2,1)} %param.8) | copy-start | bytes 1769476
  18.1 9.8 %all-to-all-start = ((bf16[8,1,37]{2,1,0:T(2,128)(2,1)}), bf16[8,1,37]{2,1,0:T(2,128)(2,1)S(1)}, u32[]{:S(2)}, u32[]{:S(2)}) async-start(bf16[8,1,37]{2,1,0:T(2,128)(2,1)} %copy.20), calls=%async_computation | async-start | bytes 8192 | tf_op jit(solution)/shard_map/all_to_all | solution.py:165
  27.9 14.8 %all-to-all-start.1 = ((bf16[8,37,1024]{2,1,0:T(8,128)(2,1)}), bf16[8,37,1024]{2,1,0:T(8,128)(2,1)S(1)}, u32[]{:S(2)}, u32[]{:S(2)}) async-start(bf16[8,37,1024]{2,1,0:T(8,128)(2,1)} %select_select_fusion.3), calls=%async_computation.1 | async-start | bytes 1310720 | tf_op jit(solution)/shard_map/all_to_all | solution.py:164
  31.6 49.3 %all-gather.2.cloned.1.call-start = ((), (), s32[]{:S(2)}) async-start(), calls=%async_computation.4 | async-start | bytes 1769472 | tf_op jit(solution)/shard_map/all_gather | solution.py:148
  50.5 26.7 %all-to-all-start.2 = ((bf16[8,37,2048]{2,1,0:T(8,128)(2,1)}), bf16[8,37,2048]{2,1,0:T(8,128)(2,1)}, u32[]{:S(2)}, u32[]{:S(2)}) async-start(bf16[8,37,2048]{2,1,0:T(8,128)(2,1)} %select_select_fusion.1), calls=%async_computation.2 | async-start | bytes 2621440 | tf_op jit(solution)/shard_map/all_to_all | solution.py:163
  85.6 1.0 copy-start.2
  85.6 1.0 copy-start.3
  87.2 2.7 %copy-start.4 = (pred[96,384]{1,0:T(8,128)(4,1)S(1)}, pred[96,384]{1,0:T(8,128)(4,1)}, u32[]{:S(2)}) copy-start(pred[96,384]{1,0:T(8,128)(4,1)} %broadcast_compare_fusion.2) | copy-start | bytes 110596 | tf_op jit(solution)/shard_map/while
  89.9 0.9 copy-start.5
  90.9 0.6 copy-start.6
  95.6 1.0 copy-start.2
  95.6 1.0 copy-start.3
  97.3 3.0 %copy-start.4 = (pred[96,384]{1,0:T(8,128)(4,1)S(1)}, pred[96,384]{1,0:T(8,128)(4,1)}, u32[]{:S(2)}) copy-start(pred[96,384]{1,0:T(8,128)(4,1)} %broadcast_compare_fusion.2) | copy-start | bytes 110596 | tf_op jit(solution)/shard_map/while
  100.3 0.9 copy-start.5
  101.3 0.6 copy-start.6
  103.3 0.9 copy-start.10
  103.8 0.7 copy-start.7
  107.4 1.7 %copy-start.8 = (pred[8,37]{1,0:T(8,128)(4,1)S(1)}, pred[8,37]{1,0:T(8,128)(4,1)}, u32[]{:S(2)}) copy-start(pred[8,37]{1,0:T(8,128)(4,1)} %get-tuple-element.192) | copy-start | bytes 892
  107.4 1.7 %copy-start.9 = (pred[8,37]{1,0:T(8,128)(4,1)S(1)}, pred[8,37]{1,0:T(8,128)(4,1)}, u32[]{:S(2)}) copy-start(pred[8,37]{1,0:T(8,128)(4,1)} %get-tuple-element.193) | copy-start | bytes 892
  110.4 22.5 %all-to-all-start.3 = ((bf16[8,37,2048]{2,1,0:T(8,128)(2,1)}), bf16[8,37,2048]{2,1,0:T(8,128)(2,1)}, u32[]{:S(2)}, u32[]{:S(2)}) async-start(bf16[8,37,2048]{2,1,0:T(8,128)(2,1)} %select_select_fusion), calls=%async_computation.3 | async-start | bytes 2621440 | tf_op jit(solution)/shard_map/all_to_all | solution.py:172
Sparse Core Ops, SparseCore 0:
  44.7 29.4 all-gather.1
where the time goes:
time: 148 us; the launch traced here: 147 us
  waiting for transfers between devices  41.7 us (28%)
  local copies, waits for them, and re-layouts  36.8 us (25%)
  other arithmetic  24.7 us (17%)
  between operations  17.7 us (12%)
  starting transfers between devices  17.6 us (12%)
  matrix products  6.97 us (5%)
    all_to_all x1, waiting for transfers between devices, per_device(): lax.all_to_all(packed[0], 'ctx', split_axis=0, concat_axis=0, tiled=True)  20.8 us
    all_to_all x1, waiting for transfers between devices, per_device(): lax.all_to_all(outgoing, 'ctx', split_axis=0, concat_axis=0, tiled=True)  16.8 us
    gather x6, local copies, waits for them, and re-layouts, pack_forward(): gathered_rows = jnp.take(member, picked, axis=0)  10.6 us
    select_n x3, other arithmetic, unpack_forward(): jnp.take(member.reshape((-1,) + member.shape[2:]), picked, axis=0)  7.14 us
    dot_general x2, matrix products, update(): jnp.einsum('kgqc,ckd->qkgd', weights.astype(jnp.bfloat16), block_value_ro...  5.74 us
    dynamic_slice x6, local copies, waits for them, and re-layouts, fold_piece(): lax.scan(scan_step, running, (blocks, jnp.arange(num_blocks, dtype=jnp.in...  5.57 us
    all_to_all x1, starting transfers between devices, per_device(): lax.all_to_all(packed[2], 'ctx', split_axis=0, concat_axis=0, tiled=True)  5.17 us
    gather x2, local copies, waits for them, and re-layouts, pack_return(): gathered_rows = jnp.take(scaled, picked, axis=0)  4.63 us
  transfers between devices with their start and end apart: 5, of which 4 were waited for; matrix products, arithmetic and copies ran while one was open for 16% of the time, Pallas kernels for 0%

commit v1 on v0

v1 whole, which is shorter than its diff:
```python
import functools
import math

import jax
import jax.numpy as jnp
from jax import lax
from jax.experimental import pallas as pl
from jax.experimental.pallas import tpu as pltpu
from jax.sharding import PartitionSpec as P

HEAD_SIZE = 128
TOK_DEV = 768
PIECES = 2
MASKED = -1e30


def kernel(
    n,
    positions_ref,
    queries_ref,
    kv_ref,
    gate_ref,
    out_ref,
    queries,
    gathered,
    placing,
    packed,
    accum,
    maxima,
    bias,
    local_sem,
    spread_send,
    spread_recv,
    share_send,
    share_recv,
    pass_send,
    pass_recv,
):
    me = lax.axis_index("ctx")
    chip, core = me // 2, lax.rem(me, 2)
    chips = n // 2
    partner = me + 1 - 2 * core
    slots = kv_ref.shape[0]
    strips = kv_ref.shape[1] // HEAD_SIZE
    kv_heads = strips // 2
    group = queries_ref.shape[1] // HEAD_SIZE // kv_heads
    total = positions_ref.shape[1]
    rows = total // (n // strips)
    piece = rows // PIECES

    def strip_of(device):
        return lax.rem(device, strips)

    def place_of(device, p):
        start = pl.multiple_of((device // strips) * rows + p * piece, 16)
        return packed.at[strip_of(device), pl.ds(start, piece), :]

    def columns(strip):
        return pl.ds(pl.multiple_of(strip * HEAD_SIZE, HEAD_SIZE), HEAD_SIZE)

    load_queries = pltpu.make_async_copy(queries_ref, queries, local_sem.at[0])
    load_queries.start()
    my_slots = pl.ds(pl.multiple_of(me * slots, 16), slots)
    keep = pltpu.make_async_copy(
        kv_ref.at[:, columns(strip_of(me))], gathered.at[my_slots, :], local_sem.at[1]
    )
    keep.start()

    barrier = pltpu.get_barrier_semaphore()
    for o in range(1, n):
        pl.semaphore_signal(
            barrier,
            inc=1,
            device_id={"ctx": lax.rem(me + o, n)},
            device_id_type=pl.DeviceIdType.MESH,
        )
    pl.semaphore_wait(barrier, n - 1)

    spread = []
    for o in range(1, n):
        target = lax.rem(me + o, n)
        copy = pltpu.make_async_remote_copy(
            src_ref=kv_ref.at[:, columns(strip_of(target))],
            dst_ref=gathered.at[my_slots, :],
            send_sem=spread_send.at[o],
            recv_sem=spread_recv.at[o],
            device_id={"ctx": target},
            device_id_type=pl.DeviceIdType.MESH,
        )
        copy.start()
        spread.append(copy)

    positions = positions_ref[...]

    def below(bound):
        hit = jnp.where(positions < bound, 1.0, 0.0)
        return jnp.sum(hit, axis=1, keepdims=True).astype(jnp.int32)

    base = (me // strips) * rows
    shard = lax.broadcasted_iota(jnp.int32, (n, 1), 0)
    starts, ends = below(shard * TOK_DEV), below((shard + 1) * TOK_DEV)
    slot = lax.broadcasted_iota(jnp.int32, (n, slots), 1)
    shift = jnp.where(slot < ends - starts, starts - base, -(2**24))
    distance = lax.broadcasted_iota(jnp.int32, (rows, slots), 0) - lax.broadcasted_iota(
        jnp.int32, (rows, slots), 1
    )
    for s in range(n):
        placing[s] = jnp.where(distance == shift[s : s + 1, :], 1.0, 0.0).astype(jnp.bfloat16)

    my_start, my_end = below(me * TOK_DEV), below((me + 1) * TOK_DEV)
    across = lax.broadcasted_iota(jnp.int32, (slots, slots), 1)
    down = lax.broadcasted_iota(jnp.int32, (slots, slots), 0)
    gate = jnp.sum(
        jnp.where(across == down, gate_ref[...].astype(jnp.float32), 0.0), axis=1, keepdims=True
    )
    live = down[:, :1] < my_end - my_start

    keep.wait()
    for copy in spread:
        copy.wait_recv()

    sends = list(spread)
    share, forward = {}, {}

    def send(p, source, target, send_sem, recv_sem):
        ref = place_of(source, p)
        copy = pltpu.make_async_remote_copy(
            src_ref=ref,
            dst_ref=ref,
            send_sem=send_sem,
            recv_sem=recv_sem,
            device_id={"ctx": target},
            device_id_type=pl.DeviceIdType.MESH,
        )
        copy.start()
        return copy

    for p in range(PIECES):
        strip = jnp.zeros((piece, HEAD_SIZE), jnp.float32)
        for s in range(n):
            strip += jnp.dot(
                placing[s, p * piece : (p + 1) * piece, :],
                gathered[s * slots : (s + 1) * slots, :],
                preferred_element_type=jnp.float32,
            )
        mine = pl.ds(pl.multiple_of(base + p * piece, 16), piece)
        packed[strip_of(me), mine, :] = strip.astype(jnp.bfloat16)
        for o in range(1, chips):
            target = lax.rem(chip + o, chips) * 2 + core
            share[p, o] = send(p, me, target, share_send.at[p, o], share_recv.at[p, o])
        share[p, 0] = send(p, me, partner, share_send.at[p, 0], share_recv.at[p, 0])

    factor = math.log2(math.e) / math.sqrt(HEAD_SIZE)
    ones = jnp.ones((piece, HEAD_SIZE), jnp.bfloat16)
    load_queries.wait()
    key_at = lax.broadcasted_iota(jnp.int32, (slots, piece), 1) - lax.broadcasted_iota(
        jnp.int32, (slots, piece), 0
    )

    def attend(start, first, last):
        bias[...] = jnp.where(key_at <= my_start - start, 0.0, MASKED)
        span = slice(start, start + piece)

        def one_head(h, carry):
            keys = packed[h, span, :]
            values = jnp.concatenate([packed[kv_heads + h, span, :], ones], axis=1)
            for g in range(group):
                head = h * group + g
                scores = lax.dot_general(
                    queries[:, columns(head)],
                    keys,
                    (((1,), (1,)), ((), ())),
                    preferred_element_type=jnp.float32,
                )
                scores = scores * factor + bias[...]
                top = jnp.max(scores, axis=1, keepdims=True)
                if not first:
                    before = maxima[head][:, :1]
                    top = jnp.maximum(top, before)
                weights = jnp.exp2(scores - top).astype(jnp.bfloat16)
                mixed = jnp.dot(weights, values, preferred_element_type=jnp.float32)
                if not first:
                    mixed += accum[head] * jnp.exp2(before - top)
                if last:
                    result = mixed[:, :HEAD_SIZE] / mixed[:, HEAD_SIZE:] * gate
                    out_ref[:, columns(head)] = jnp.where(live, result, 0.0).astype(out_ref.dtype)
                else:
                    accum[head] = mixed
                    maxima[head] = jnp.broadcast_to(top, (slots, HEAD_SIZE))
            return carry

        lax.fori_loop(0, kv_heads, one_head, 0)

    for p in range(PIECES):
        for o in range(1, chips):
            share[p, o].wait_recv()
            source = lax.rem(chip + chips - o, chips) * 2 + core
            forward[p, o] = send(p, source, partner, pass_send.at[p, o], pass_recv.at[p, o])
        share[p, 0].wait_recv()
        for o in range(1, chips):
            forward[p, o].wait_recv()
        parts = n // strips
        for r in range(parts):
            attend(
                r * rows + p * piece,
                first=p == 0 and r == 0,
                last=p == PIECES - 1 and r == parts - 1,
            )

    for copy in sends + list(share.values()) + list(forward.values()):
        copy.wait_send()


def per_device(n, positions, queries, keys_values, router_weight):
    slots, width = queries.shape
    total = positions.shape[0]
    strips = keys_values.shape[1] // HEAD_SIZE
    rows = total // (n // strips)
    piece = rows // PIECES
    heads = width // HEAD_SIZE
    chips = n // 2
    vmem = pl.BlockSpec(memory_space=pltpu.VMEM)
    anywhere = pl.BlockSpec(memory_space=pl.ANY)
    dma = pltpu.SemaphoreType.DMA
    return pl.pallas_call(
        functools.partial(kernel, n),
        out_shape=jax.ShapeDtypeStruct((slots, width), jnp.bfloat16),
        in_specs=[vmem, anywhere, anywhere, vmem],
        out_specs=vmem,
        scratch_shapes=[
            pltpu.VMEM((slots, width), jnp.bfloat16),
            pltpu.VMEM((n * slots, HEAD_SIZE), jnp.bfloat16),
            pltpu.VMEM((n, rows, slots), jnp.bfloat16),
            pltpu.VMEM((strips, total, HEAD_SIZE), jnp.bfloat16),
            pltpu.VMEM((heads, slots, 2 * HEAD_SIZE), jnp.float32),
            pltpu.VMEM((heads, slots, HEAD_SIZE), jnp.float32),
            pltpu.VMEM((slots, piece), jnp.float32),
            dma((2,)),
            dma((n,)),
            dma((n,)),
            dma((PIECES, chips)),
            dma((PIECES, chips)),
            dma((PIECES, chips)),
            dma((PIECES, chips)),
        ],
        compiler_params=pltpu.CompilerParams(
            collective_id=0, has_side_effects=True, vmem_limit_bytes=56 * 2**20
        ),
        cost_estimate=pl.CostEstimate(
            flops=4 * slots * total * width,
            bytes_accessed=4 * slots * width + 2 * total * strips * HEAD_SIZE,
            transcendentals=slots * total * heads,
        ),
    )(positions.reshape(1, total), queries, keys_values, router_weight.reshape(1, slots))


def solution(mesh):
    in_specs = (P("dp"), P(("dp", "ctx"), None), P(("dp", "ctx"), None), P(("dp", "ctx")))
    out_specs = P(("dp", "ctx"), None)
    return jax.shard_map(
        functools.partial(per_device, mesh.shape["ctx"]),
        mesh=mesh,
        in_specs=in_specs,
        out_specs=out_specs,
        check_vma=False,
    )
```

time: 148 us -> 38.8 us (0.26)
  waiting for transfers between devices: 41.7 us -> 0 us
  Pallas kernels: 0 us -> 33.5 us
  local copies, waits for them, and re-layouts: 36.8 us -> 4.93 us
  other arithmetic: 24.7 us -> 0 us
  between operations: 17.7 us -> 0.01 us
  starting transfers between devices: 17.6 us -> 0 us
  matrix products: 6.97 us -> 0 us
    all_to_all x4 -> x0, waiting for transfers between devices: 41.7 us -> none  [the longest x1 20.8 us: per_device(): lax.all_to_all(packed[0], 'ctx', split_axis=0, concat_axis=0, tiled=True)]
    pallas_call x0 -> x1, Pallas kernels: none -> 33.5 us  [per_device(): pl.pallas_call(functools.partial(kernel, n), out_shape=jax.ShapeDtypeStru...]
    gather x14 -> x0, local copies, waits for them, and re-layouts: 22.1 us -> none  [the longest x6 10.6 us: pack_forward(): gathered_rows = jnp.take(member, picked, axis=0)]
    all_to_all x4 -> x0, starting transfers between devices: 17.6 us -> none  [the longest x1 5.17 us: per_device(): lax.all_to_all(packed[2], 'ctx', split_axis=0, concat_axis=0, tiled=True)]
    select_n x11 -> x0, other arithmetic: 14.7 us -> none  [the longest x3 7.14 us: unpack_forward(): jnp.take(member.reshape((-1,) + member.shape[2:]), picked, axis=0)]
    dot_general x4 -> x0, matrix products: 6.97 us -> none  [the longest x2 5.74 us: update(): jnp.einsum('kgqc,ckd->qkgd', weights.astype(jnp.bfloat16), block_value_ro...]
    dynamic_slice x6 -> x0, local copies, waits for them, and re-layouts: 5.57 us -> none  [fold_piece(): lax.scan(scan_step, running, (blocks, jnp.arange(num_blocks, dtype=jnp.in...]
    reduce_sum x4 -> x0, other arithmetic: 2.92 us -> none  [the longest x2 1.84 us: update(): total_new = total_run * factor + jnp.sum(weights, axis=-1)]
  transfers between devices with their start and end apart: 5 -> 0, of which waited for: 4 -> 0; matrix products, arithmetic and copies ran while one was open for 16% -> 0% of each run, Pallas kernels for 0% -> 0%
where the time goes in v1:
time: 38.8 us; the launch traced here: 38.4 us
  Pallas kernels  33.5 us (86%)
  local copies, waits for them, and re-layouts  4.93 us (13%)
    pallas_call x1, Pallas kernels, per_device(): pl.pallas_call(functools.partial(kernel, n), out_shape=jax.ShapeDtypeStru...  33.5 us
    unnamed x1, local copies, waits for them, and re-layouts  2.41 us
    reshape x1, local copies, waits for them, and re-layouts, per_device(): positions.reshape(1, total)  1.27 us
    reshape x1, local copies, waits for them, and re-layouts, per_device(): router_weight.reshape(1, slots)  1.25 us

profile of v1, /device:TPU:0, one launch (start us, length us, event | category | flops | bytes accessed | tf_op | source)
XLA Modules:
  0.0 38.4 jit_solution(3758182721120642582)
XLA Ops:
  0.0 1.3 %reshape.7.gate_ref = bf16[1,288]{1,0:T(2,128)(2,1)} reshape(bf16[288]{0:T(512)(128)(2,1)} %param.7) | data formatting | bytes 1152 | tf_op jit(solution)/shard_map/reshape | solution.py:254
  1.3 1.3 %reshape.6.positions_ref = s32[1,768]{1,0:T(1,128)} reshape(s32[768]{0:T(1024)} %param.4) | data formatting | bytes 6144 | tf_op jit(solution)/shard_map/reshape | solution.py:254
  2.5 33.5 %shard_map.46 = bf16[288,2048]{1,0:T(8,128)(2,1)} custom-call(s32[1,768]{1,0:T(1,128)} %reshape.6.positions_ref, bf16[288,2048]{1,0:T(8,128)(2,1)} %queries_ref.1, bf16[288,1024]{1,0:T(8,128)(2,1)} %kv_ref.1, bf16[1,288]{1,0:T(2,128)(2,1)} %reshape.7.gate_ref), custom_call_target="tpu_custom_call" | custom-call | flops 1811939328 | bytes 3932160 | tf_op jit(solution)/shard_map/pallas_call | solution.py:225
  36.0 2.4 %copy.6 = bf16[288,2048]{1,0:T(8,128)(2,1)} copy(bf16[288,2048]{1,0:T(8,128)(2,1)} %shard_map.46) | data formatting | bytes 2359296

commit v2 on v1

--- a/solution.py
+++ b/solution.py
@@ -43,8 +43,9 @@
     slots = kv_ref.shape[0]
     strips = kv_ref.shape[1] // HEAD_SIZE
     kv_heads = strips // 2
-    group = queries_ref.shape[1] // HEAD_SIZE // kv_heads
-    total = positions_ref.shape[1]
+    heads = queries_ref.shape[1] // HEAD_SIZE
+    group = heads // kv_heads
+    total = positions_ref.shape[0]
     rows = total // (n // strips)
     piece = rows // PIECES
 
@@ -58,11 +59,13 @@
     def columns(strip):
         return pl.ds(pl.multiple_of(strip * HEAD_SIZE, HEAD_SIZE), HEAD_SIZE)
 
-    load_queries = pltpu.make_async_copy(queries_ref, queries, local_sem.at[0])
-    load_queries.start()
+    load_queries = [
+        pltpu.make_async_copy(queries_ref.at[:, columns(i)], queries.at[i], local_sem.at[i])
+        for i in range(heads)
+    ]
     my_slots = pl.ds(pl.multiple_of(me * slots, 16), slots)
     keep = pltpu.make_async_copy(
-        kv_ref.at[:, columns(strip_of(me))], gathered.at[my_slots, :], local_sem.at[1]
+        kv_ref.at[:, columns(strip_of(me))], gathered.at[my_slots, :], local_sem.at[heads]
     )
     keep.start()
 
@@ -89,8 +92,10 @@
         )
         copy.start()
         spread.append(copy)
-
-    positions = positions_ref[...]
+    for copy in load_queries:
+        copy.start()
+
+    positions = positions_ref[...].reshape(1, total)
 
     def below(bound):
         hit = jnp.where(positions < bound, 1.0, 0.0)
@@ -111,7 +116,7 @@
     across = lax.broadcasted_iota(jnp.int32, (slots, slots), 1)
     down = lax.broadcasted_iota(jnp.int32, (slots, slots), 0)
     gate = jnp.sum(
-        jnp.where(across == down, gate_ref[...].astype(jnp.float32), 0.0), axis=1, keepdims=True
+        jnp.where(across == down, gate_ref[...].astype(jnp.float32).reshape(1, slots), 0.0), axis=1, keepdims=True
     )
     live = down[:, :1] < my_end - my_start
 
@@ -152,7 +157,8 @@
 
     factor = math.log2(math.e) / math.sqrt(HEAD_SIZE)
     ones = jnp.ones((piece, HEAD_SIZE), jnp.bfloat16)
-    load_queries.wait()
+    for copy in load_queries:
+        copy.wait()
     key_at = lax.broadcasted_iota(jnp.int32, (slots, piece), 1) - lax.broadcasted_iota(
         jnp.int32, (slots, piece), 0
     )
@@ -164,29 +170,32 @@
         def one_head(h, carry):
             keys = packed[h, span, :]
             values = jnp.concatenate([packed[kv_heads + h, span, :], ones], axis=1)
-            for g in range(group):
-                head = h * group + g
-                scores = lax.dot_general(
-                    queries[:, columns(head)],
-                    keys,
-                    (((1,), (1,)), ((), ())),
-                    preferred_element_type=jnp.float32,
-                )
-                scores = scores * factor + bias[...]
-                top = jnp.max(scores, axis=1, keepdims=True)
-                if not first:
-                    before = maxima[head][:, :1]
-                    top = jnp.maximum(top, before)
-                weights = jnp.exp2(scores - top).astype(jnp.bfloat16)
-                mixed = jnp.dot(weights, values, preferred_element_type=jnp.float32)
-                if not first:
-                    mixed += accum[head] * jnp.exp2(before - top)
-                if last:
-                    result = mixed[:, :HEAD_SIZE] / mixed[:, HEAD_SIZE:] * gate
-                    out_ref[:, columns(head)] = jnp.where(live, result, 0.0).astype(out_ref.dtype)
-                else:
-                    accum[head] = mixed
-                    maxima[head] = jnp.broadcast_to(top, (slots, HEAD_SIZE))
+            mine = pl.ds(h * group, group)
+            scores = lax.dot_general(
+                queries[mine].reshape(group * slots, HEAD_SIZE),
+                keys,
+                (((1,), (1,)), ((), ())),
+                preferred_element_type=jnp.float32,
+            )
+            scores = scores.reshape(group, slots, piece) * factor + bias[...]
+            top = jnp.max(scores, axis=2, keepdims=True)
+            if not first:
+                before = maxima[mine][:, :, :1]
+                top = jnp.maximum(top, before)
+            weights = jnp.exp2(scores - top).astype(jnp.bfloat16)
+            mixed = jnp.dot(
+                weights.reshape(group * slots, piece), values, preferred_element_type=jnp.float32
+            ).reshape(group, slots, 2 * HEAD_SIZE)
+            if not first:
+                mixed += accum[mine] * jnp.exp2(before - top)
+            if last:
+                result = mixed[:, :, :HEAD_SIZE] / mixed[:, :, HEAD_SIZE:] * gate
+                result = jnp.where(live, result, 0.0).astype(out_ref.dtype)
+                for g in range(group):
+                    out_ref[:, columns(h * group + g)] = result[g]
+            else:
+                accum[mine] = mixed
+                maxima[mine] = jnp.broadcast_to(top, (group, slots, HEAD_SIZE))
             return carry
 
         lax.fori_loop(0, kv_heads, one_head, 0)
@@ -211,6 +220,12 @@
         copy.wait_send()
 
 
+def write_out(attended_ref, out_ref, sem):
+    copy = pltpu.make_async_copy(attended_ref, out_ref, sem)
+    copy.start()
+    copy.wait()
+
+
 def per_device(n, positions, queries, keys_values, router_weight):
     slots, width = queries.shape
     total = positions.shape[0]
@@ -222,20 +237,20 @@
     vmem = pl.BlockSpec(memory_space=pltpu.VMEM)
     anywhere = pl.BlockSpec(memory_space=pl.ANY)
     dma = pltpu.SemaphoreType.DMA
-    return pl.pallas_call(
+    attended = pl.pallas_call(
         functools.partial(kernel, n),
         out_shape=jax.ShapeDtypeStruct((slots, width), jnp.bfloat16),
         in_specs=[vmem, anywhere, anywhere, vmem],
         out_specs=vmem,
         scratch_shapes=[
-            pltpu.VMEM((slots, width), jnp.bfloat16),
+            pltpu.VMEM((heads, slots, HEAD_SIZE), jnp.bfloat16),
             pltpu.VMEM((n * slots, HEAD_SIZE), jnp.bfloat16),
             pltpu.VMEM((n, rows, slots), jnp.bfloat16),
             pltpu.VMEM((strips, total, HEAD_SIZE), jnp.bfloat16),
             pltpu.VMEM((heads, slots, 2 * HEAD_SIZE), jnp.float32),
             pltpu.VMEM((heads, slots, HEAD_SIZE), jnp.float32),
             pltpu.VMEM((slots, piece), jnp.float32),
-            dma((2,)),
+            dma((heads + 1,)),
             dma((n,)),
             dma((n,)),
             dma((PIECES, chips)),
@@ -251,7 +266,15 @@
             bytes_accessed=4 * slots * width + 2 * total * strips * HEAD_SIZE,
             transcendentals=slots * total * heads,
         ),
-    )(positions.reshape(1, total), queries, keys_values, router_weight.reshape(1, slots))
+    )(positions, queries, keys_values, router_weight)
+
+    return pl.pallas_call(
+        write_out,
+        out_shape=jax.ShapeDtypeStruct((slots, width), jnp.bfloat16),
+        in_specs=[anywhere],
+        out_specs=anywhere,
+        scratch_shapes=[dma],
+    )(attended)
 
 
 def solution(mesh):

time: 38.8 us -> 70.5 us (1.82)
  Pallas kernels: 33.5 us -> 70.1 us
  local copies, waits for them, and re-layouts: 4.93 us -> 0 us
    pallas_call x0 -> x1, Pallas kernels: none -> 36.8 us  [per_device(): pl.pallas_call(write_out, out_shape=jax.ShapeDtypeStruct((slots, width),...]
    reshape x2 -> x0, local copies, waits for them, and re-layouts: 2.52 us -> none  [the longest x1 1.27 us: per_device(): positions.reshape(1, total)]
    unnamed x1 -> x0, local copies, waits for them, and re-layouts: 2.41 us -> none
where the time goes in v2:
time: 70.5 us; the launch traced here: 70.1 us
  Pallas kernels  70.1 us (99%)
    pallas_call x1, Pallas kernels, per_device(): pl.pallas_call(write_out, out_shape=jax.ShapeDtypeStruct((slots, width),...  36.8 us
    pallas_call x1, Pallas kernels, per_device(): pl.pallas_call(functools.partial(kernel, n), out_shape=jax.ShapeDtypeStru...  33.3 us

profile of v2, /device:TPU:0, one launch (start us, length us, event | category | flops | bytes accessed | tf_op | source)
XLA Modules:
  0.0 70.1 jit_solution(12717405968732242943)
XLA Ops:
  0.0 33.3 %shard_map.46.attended_ref = bf16[288,2048]{1,0:T(8,128)(2,1)} custom-call(s32[768]{0:T(1024)} %positions_ref.1, bf16[288,2048]{1,0:T(8,128)(2,1)} %queries_ref.1, bf16[288,1024]{1,0:T(8,128)(2,1)} %kv_ref.1, bf16[288]{0:T(512)(128)(2,1)} %gate_ref.1), custom_call_target="tpu_custom_call" | custom-call | flops 1811939328 | bytes 3932160 | tf_op jit(solution)/shard_map/pallas_call | solution.py:240
  33.3 36.8 %shard_map.47 = bf16[288,2048]{1,0:T(8,128)(2,1)} custom-call(bf16[288,2048]{1,0:T(8,128)(2,1)} %shard_map.46.attended_ref), custom_call_target="tpu_custom_call" | custom-call | tf_op jit(solution)/shard_map/pallas_call | solution.py:271

commit v3 on v2

--- a/solution.py
+++ b/solution.py
@@ -220,10 +220,22 @@
         copy.wait_send()
 
 
-def write_out(attended_ref, out_ref, sem):
-    copy = pltpu.make_async_copy(attended_ref, out_ref, sem)
-    copy.start()
-    copy.wait()
+def write_out(parts, attended_ref, out_ref, held, load_sem, store_sem):
+    size = attended_ref.shape[0] // parts
+    loads, stores = [], []
+    for i in range(parts):
+        span = pl.ds(i * size, size)
+        loads.append(
+            pltpu.make_async_copy(attended_ref.at[span], held.at[span], load_sem.at[i])
+        )
+        stores.append(pltpu.make_async_copy(held.at[span], out_ref.at[span], store_sem.at[i]))
+    for copy in loads:
+        copy.start()
+    for load, store in zip(loads, stores):
+        load.wait()
+        store.start()
+    for copy in stores:
+        copy.wait()
 
 
 def per_device(n, positions, queries, keys_values, router_weight):
@@ -268,12 +280,17 @@
         ),
     )(positions, queries, keys_values, router_weight)
 
+    parts = math.gcd(slots // 16, 6)
     return pl.pallas_call(
-        write_out,
+        functools.partial(write_out, parts),
         out_shape=jax.ShapeDtypeStruct((slots, width), jnp.bfloat16),
         in_specs=[anywhere],
         out_specs=anywhere,
-        scratch_shapes=[dma],
+        scratch_shapes=[
+            pltpu.VMEM((slots, width), jnp.bfloat16),
+            dma((parts,)),
+            dma((parts,)),
+        ],
     )(attended)
 
 

time: 70.5 us -> 35.7 us (0.51)
  Pallas kernels: 70.1 us -> 35.4 us
    pallas_call x1, Pallas kernels: 36.8 us -> 2.13 us  [per_device(): pl.pallas_call(functools.partial(write_out, parts), out_shape=jax.ShapeDt...]
where the time goes in v3:
time: 35.7 us; the launch traced here: 35.4 us
  Pallas kernels  35.4 us (99%)
    pallas_call x1, Pallas kernels, per_device(): pl.pallas_call(functools.partial(kernel, n), out_shape=jax.ShapeDtypeStru...  33.3 us
    pallas_call x1, Pallas kernels, per_device(): pl.pallas_call(functools.partial(write_out, parts), out_shape=jax.ShapeDt...  2.13 us

profile of v3, /device:TPU:0, one launch (start us, length us, event | category | flops | bytes accessed | tf_op | source)
XLA Modules:
  0.0 35.4 jit_solution(9546345443056976449)
XLA Ops:
  0.0 33.3 %shard_map.46.attended_ref = bf16[288,2048]{1,0:T(8,128)(2,1)} custom-call(s32[768]{0:T(1024)} %positions_ref.1, bf16[288,2048]{1,0:T(8,128)(2,1)} %queries_ref.1, bf16[288,1024]{1,0:T(8,128)(2,1)} %kv_ref.1, bf16[288]{0:T(512)(128)(2,1)} %gate_ref.1), custom_call_target="tpu_custom_call" | custom-call | flops 1811939328 | bytes 3932160 | tf_op jit(solution)/shard_map/pallas_call | solution.py:252
  33.3 2.1 %shard_map.47 = bf16[288,2048]{1,0:T(8,128)(2,1)} custom-call(bf16[288,2048]{1,0:T(8,128)(2,1)} %shard_map.46.attended_ref), custom_call_target="tpu_custom_call" | custom-call | tf_op jit(solution)/shard_map/pallas_call | solution.py:284
